TPU v7x, 32 devices: a whole 2x2x4 slice. The times are simulated.
32 devices in a mesh: seq: 16 (over z, x, core), mem: 2 (over y).
Axes of the slice: x: 2, y: 2, z: 4, core: 2. Of those that a mesh axis runs over, the one named last changes fastest.
Arguments:
- inputs: bfloat16 [4096, 1024], P('seq'), may hold values from -6 to 6
- memory: bfloat16 [64, 128, 1024], P('seq', 'mem'), may hold values from -6 to 6
- cotangent: bfloat16 [4096, 1024], P('seq'), may hold values from -6 to 6
- is_long: int32 [16], P('seq'), may hold values from 0 to 1, as said below
- memory_len: int32 [64], P('seq'), may hold values from 0 to 128, as said below
- distance_bucket: int32 [256], replicated, may hold values from 0 to 31, as said below
- norm_self: float32 [1024], replicated, may hold values from 0.5 to 1.5
- query_self: bfloat16 [1024, 1024], replicated, may hold values from -0.046875 to 0.046875
- key_self: bfloat16 [1024, 512], replicated, may hold values from -0.1875 to 0.1875
- value_self: bfloat16 [1024, 512], replicated, may hold values from -0.1875 to 0.1875
- output_self: bfloat16 [1024, 1024], replicated, may hold values from -0.5 to 0.5
- bias_table: float32 [32, 16], replicated, may hold values from -4 to 4
- norm_cross: float32 [1024], replicated, may hold values from 0.5 to 1.5
- query_cross: bfloat16 [1024, 1024], replicated, may hold values from -0.046875 to 0.046875
- key_cross: bfloat16 [1024, 512], replicated, may hold values from -0.1875 to 0.1875
- value_cross: bfloat16 [1024, 512], replicated, may hold values from -0.1875 to 0.1875
- output_cross: bfloat16 [1024, 1024], replicated, may hold values from -0.5 to 0.5
- norm_feed: float32 [1024], replicated, may hold values from 0.5 to 1.5
- gate_proj: bfloat16 [1024, 2816], replicated, may hold values from -0.1875 to 0.1875
- up_proj: bfloat16 [1024, 2816], replicated, may hold values from -0.1875 to 0.1875
- down_proj: bfloat16 [2816, 1024], replicated, may hold values from -0.109375 to 0.109375
Outputs:
- outputs: bfloat16 [4096, 1024], P('seq')
- inputs_grad: float32 [4096, 1024], P('seq')
- memory_grad: float32 [64, 128, 1024], P('seq', 'mem')
- norm_self_grad: float32 [1024], P('seq')
- query_self_grad: float32 [1024, 1024], P('seq')
- key_self_grad: float32 [1024, 512], P('seq')
- value_self_grad: float32 [1024, 512], P('seq')
- output_self_grad: float32 [1024, 1024], P('seq')
- bias_table_grad: float32 [32, 16], replicated
- norm_cross_grad: float32 [1024], P('seq')
- query_cross_grad: float32 [1024, 1024], P('seq')
- key_cross_grad: float32 [1024, 512], P(('seq', 'mem'))
- value_cross_grad: float32 [1024, 512], P(('seq', 'mem'))
- output_cross_grad: float32 [1024, 1024], P('seq')
- norm_feed_grad: float32 [1024], P('seq')
- gate_proj_grad: float32 [1024, 2816], P('seq')
- up_proj_grad: float32 [1024, 2816], P('seq')
- down_proj_grad: float32 [2816, 1024], P('seq')
Inputs may be any that keep to these rules, and one draw needn't show every extreme that they name: `is_long`: exactly 5 entries are 1, the others 0. `memory_len`: entry 4 * i + s belongs to slot s of group i. Where is_long[i] is 1, slot 0 holds more than 64 positions and the other slots 0; elsewhere every slot holds more than 64. Some slot 0 holds exactly 128. `distance_bucket`: entry d is the bucket of distance d: d itself below 16, never falling, rising by at most one from one distance to the next, and 31 at distance 256 - 1.
All inputs are finite; a program needn't handle non-finite values.
Results may differ from a plain program's by a relative error of at most 0.02.
The roundings to bfloat16 on the way count: a program that leaves them out, or rounds other values in their place, can miss the bound.
Values may be sent and summed in bfloat16 or wider, within the bound.
A program may use at most 256 MiB of HBM per device.

v0:
```python
import jax
import jax.numpy as jnp
from jax import lax
from jax.sharding import PartitionSpec as P

HEAD_DIM = 64
BUCKETS = 32
SHORT = 64
SLOTS = 4


HIGHEST = lax.Precision.HIGHEST
epsilon = 1e-06
masked_value = -1e30


def norm_forward(values, gain):
    scaling = lax.rsqrt(jnp.mean(values * values, axis=-1, keepdims=True) + epsilon)
    return (values * scaling * gain, scaling)


def norm_backward(values, scaling, gain, upstream):
    normed = values * scaling
    scaled = upstream * gain
    through = scaling * (scaled - normed * jnp.mean(scaled * normed, axis=-1, keepdims=True))
    return (through, upstream * normed)


def back_product(left_side, weight):
    return lax.dot_general(
        left_side, weight, (((1,), (1,)), ((), ())), preferred_element_type=jnp.float32
    )


def attend(queries, keys, values, bias_block, allowed):
    scores = (
        jnp.einsum("skrd,ukd->krsu", queries, keys, preferred_element_type=jnp.float32) + bias_block
    )
    scores = jnp.where(allowed, scores, masked_value)
    largest = jnp.max(scores, axis=-1, keepdims=True)
    weights = jnp.exp(scores - largest)
    totals = jnp.sum(weights, axis=-1, keepdims=True)
    attention = (weights / totals).astype(jnp.bfloat16)
    result = jnp.einsum("krsu,ukd->skrd", attention, values, preferred_element_type=jnp.float32)
    return (result, largest + jnp.log(totals))


def attend_back(queries, keys, values, bias_block, allowed, logsum, upstream):
    scores = (
        jnp.einsum("skrd,ukd->krsu", queries, keys, preferred_element_type=jnp.float32) + bias_block
    )
    scores = jnp.where(allowed, scores, masked_value)
    attention = jnp.exp(scores - logsum)
    rounded = attention.astype(jnp.bfloat16)
    values_grad = jnp.einsum(
        "krsu,skrd->ukd", rounded, upstream, preferred_element_type=jnp.float32
    )
    weights_grad = jnp.einsum(
        "skrd,ukd->krsu", upstream, values, preferred_element_type=jnp.float32
    )
    inner = jnp.sum(attention * weights_grad, axis=-1, keepdims=True)
    scores_grad = (attention * (weights_grad - inner)).astype(jnp.bfloat16)
    queries_grad = jnp.einsum(
        "krsu,ukd->skrd", scores_grad, keys, preferred_element_type=jnp.float32
    )
    keys_grad = jnp.einsum(
        "krsu,skrd->ukd", scores_grad, queries, preferred_element_type=jnp.float32
    )
    return (queries_grad.astype(jnp.bfloat16), keys_grad, values_grad, scores_grad)


def add_slot(stack, addend, slot_index):
    current = lax.dynamic_index_in_dim(stack, slot_index, 0, keepdims=False)
    return lax.dynamic_update_index_in_dim(stack, current + addend, slot_index, 0)


def shards(
    inputs,
    memory,
    cotangent,
    is_long,
    memory_len,
    distance_bucket,
    norm_self,
    query_self,
    key_self,
    value_self,
    output_self,
    bias_table,
    norm_cross,
    query_cross,
    key_cross,
    value_cross,
    output_cross,
    norm_feed,
    gate_proj,
    up_proj,
    down_proj,
):
    targets, model_width = inputs.shape
    pair_width = key_self.shape[1]
    key_heads = pair_width // HEAD_DIM
    group_size = query_self.shape[1] // pair_width
    head_count = key_heads * group_size
    long_flag = is_long[0]
    seq_span = jnp.where(long_flag == 1, targets, SHORT)
    columns = jnp.arange(targets)

    def weight_gradient(left_side, right_side):
        return lax.dot_general(
            left_side, right_side, (((0,), (0,)), ((), ())), preferred_element_type=jnp.float32
        )

    inputs_wide = inputs.astype(jnp.float32)
    normed_one, scaling_one = norm_forward(inputs_wide, norm_self)
    hidden_one = normed_one.astype(jnp.bfloat16)
    queries = (
        jnp.dot(hidden_one, query_self, preferred_element_type=jnp.float32)
        .astype(jnp.bfloat16)
        .reshape(targets, key_heads, group_size, HEAD_DIM)
    )
    keys_self = (
        jnp.dot(hidden_one, key_self, preferred_element_type=jnp.float32)
        .astype(jnp.bfloat16)
        .reshape(targets, key_heads, HEAD_DIM)
    )
    values_self = (
        jnp.dot(hidden_one, value_self, preferred_element_type=jnp.float32)
        .astype(jnp.bfloat16)
        .reshape(targets, key_heads, HEAD_DIM)
    )
    bucket_range = jnp.arange(BUCKETS)

    def self_terms(block_index):
        query_rows = block_index * SHORT + jnp.arange(SHORT)
        distance = query_rows[:, None] - columns[None, :]
        clipped = jnp.clip(distance, 0, targets - 1)
        pair_onehot = (distance_bucket[clipped][:, :, None] == bucket_range[None, None, :]).astype(
            jnp.float32
        )
        bias_block = jnp.einsum("sub,bh->hsu", pair_onehot, bias_table, precision=HIGHEST).reshape(
            key_heads, group_size, SHORT, targets
        )
        allowed = (distance >= 0) & (
            query_rows[:, None] // seq_span == columns[None, :] // seq_span
        )
        return (bias_block, allowed, pair_onehot)

    self_parts = []
    self_logsum = []
    for block_index in range(SLOTS):
        bias_block, allowed, pair_onehot = self_terms(block_index)
        lower = block_index * SHORT
        result, logsum = attend(
            queries[lower : lower + SHORT], keys_self, values_self, bias_block, allowed
        )
        self_parts.append(result)
        self_logsum.append(logsum)
    attended = (
        jnp.concatenate(self_parts, axis=0).reshape(targets, model_width).astype(jnp.bfloat16)
    )
    after_self = inputs_wide + jnp.dot(attended, output_self, preferred_element_type=jnp.float32)
    normed_two, scaling_two = norm_forward(after_self, norm_cross)
    hidden_two = normed_two.astype(jnp.bfloat16)
    cross_queries = (
        jnp.dot(hidden_two, query_cross, preferred_element_type=jnp.float32)
        .astype(jnp.bfloat16)
        .reshape(targets, key_heads, group_size, HEAD_DIM)
    )
    memory_rows = memory.reshape(-1, model_width)
    own_keys = (
        jnp.dot(memory_rows, key_cross, preferred_element_type=jnp.float32)
        .astype(jnp.bfloat16)
        .reshape(SLOTS, -1, pair_width)
    )
    own_values = (
        jnp.dot(memory_rows, value_cross, preferred_element_type=jnp.float32)
        .astype(jnp.bfloat16)
        .reshape(SLOTS, -1, pair_width)
    )
    gathered_keys, gathered_values = (
        lax.all_gather(own_keys, "mem", axis=1, tiled=True),
        lax.all_gather(own_values, "mem", axis=1, tiled=True),
    )
    slot_width = gathered_keys.shape[1]
    gathered_keys = gathered_keys.reshape(SLOTS, slot_width, key_heads, HEAD_DIM)
    gathered_values = gathered_values.reshape(SLOTS, slot_width, key_heads, HEAD_DIM)
    positions = jnp.arange(slot_width)

    def cross_terms(block_index):
        slot_index = jnp.where(long_flag == 1, 0, block_index)
        slot_keys = lax.dynamic_index_in_dim(gathered_keys, slot_index, 0, keepdims=False)
        slot_values = lax.dynamic_index_in_dim(gathered_values, slot_index, 0, keepdims=False)
        valid_count = lax.dynamic_index_in_dim(memory_len, slot_index, 0, keepdims=False)
        return (slot_index, slot_keys, slot_values, positions[None, :] < valid_count)

    cross_parts = []
    cross_logsum = []
    for block_index in range(SLOTS):
        slot_index, slot_keys, slot_values, valid = cross_terms(block_index)
        lower = block_index * SHORT
        result, logsum = attend(
            cross_queries[lower : lower + SHORT], slot_keys, slot_values, 0.0, valid
        )
        cross_parts.append(result)
        cross_logsum.append(logsum)
    cross_attended = (
        jnp.concatenate(cross_parts, axis=0).reshape(targets, model_width).astype(jnp.bfloat16)
    )
    after_cross = after_self + jnp.dot(
        cross_attended, output_cross, preferred_element_type=jnp.float32
    )
    normed_three, scaling_three = norm_forward(after_cross, norm_feed)
    hidden_three = normed_three.astype(jnp.bfloat16)
    gate_values = jnp.dot(hidden_three, gate_proj, preferred_element_type=jnp.float32)
    up_values = jnp.dot(hidden_three, up_proj, preferred_element_type=jnp.float32)
    activated = (jax.nn.gelu(gate_values, approximate=True) * up_values).astype(jnp.bfloat16)
    outputs = (
        after_cross + jnp.dot(activated, down_proj, preferred_element_type=jnp.float32)
    ).astype(jnp.bfloat16)
    upstream = cotangent.astype(jnp.float32)
    down_grad = upstream.astype(jnp.bfloat16)
    down_proj_grad = weight_gradient(activated, down_grad)
    activated_grad = back_product(down_grad, down_proj)
    _, gelu_backward = jax.vjp(
        lambda gate_in, up_in: jax.nn.gelu(gate_in, approximate=True) * up_in,
        gate_values,
        up_values,
    )
    gate_grad, up_grad = gelu_backward(activated_grad)
    gate_grad = gate_grad.astype(jnp.bfloat16)
    up_grad = up_grad.astype(jnp.bfloat16)
    gate_proj_grad = weight_gradient(hidden_three, gate_grad)
    up_proj_grad = weight_gradient(hidden_three, up_grad)
    three_grad = back_product(gate_grad, gate_proj) + back_product(up_grad, up_proj)
    through_three, gain_three = norm_backward(after_cross, scaling_three, norm_feed, three_grad)
    norm_feed_grad = jnp.sum(gain_three, axis=0)
    cross_grad = upstream + through_three
    cross_branch = cross_grad.astype(jnp.bfloat16)
    output_cross_grad = weight_gradient(cross_attended, cross_branch)
    cross_out_grad = (
        back_product(cross_branch, output_cross)
        .astype(jnp.bfloat16)
        .reshape(targets, key_heads, group_size, HEAD_DIM)
    )
    memory_keys_grad = jnp.zeros((SLOTS, slot_width, key_heads, HEAD_DIM), jnp.float32)
    memory_values_grad = jnp.zeros((SLOTS, slot_width, key_heads, HEAD_DIM), jnp.float32)
    cross_query_parts = []
    for block_index in range(SLOTS):
        slot_index, slot_keys, slot_values, valid = cross_terms(block_index)
        lower = block_index * SHORT
        query_part, keys_part, values_part, _ = attend_back(
            cross_queries[lower : lower + SHORT],
            slot_keys,
            slot_values,
            0.0,
            valid,
            cross_logsum[block_index],
            cross_out_grad[lower : lower + SHORT],
        )
        cross_query_parts.append(query_part)
        memory_keys_grad = add_slot(memory_keys_grad, keys_part, slot_index)
        memory_values_grad = add_slot(memory_values_grad, values_part, slot_index)
    cross_query_grad = jnp.concatenate(cross_query_parts, axis=0).reshape(targets, model_width)
    query_cross_grad = weight_gradient(hidden_two, cross_query_grad)
    two_grad = back_product(cross_query_grad, query_cross)
    through_two, gain_two = norm_backward(after_self, scaling_two, norm_cross, two_grad)
    norm_cross_grad = jnp.sum(gain_two, axis=0)
    after_grad = cross_grad + through_two
    own_width = own_keys.shape[1]
    own_start = lax.axis_index("mem") * own_width
    own_keys_grad = (
        lax.dynamic_slice_in_dim(memory_keys_grad, own_start, own_width, 1)
        .astype(jnp.bfloat16)
        .reshape(-1, pair_width)
    )
    own_values_grad = (
        lax.dynamic_slice_in_dim(memory_values_grad, own_start, own_width, 1)
        .astype(jnp.bfloat16)
        .reshape(-1, pair_width)
    )
    memory_grad = (
        back_product(own_keys_grad, key_cross) + back_product(own_values_grad, value_cross)
    ).reshape(memory.shape)
    key_cross_grad = lax.dot_general(
        memory_rows, own_keys_grad, (((0,), (0,)), ((), ())), preferred_element_type=jnp.float32
    )
    value_cross_grad = lax.dot_general(
        memory_rows, own_values_grad, (((0,), (0,)), ((), ())), preferred_element_type=jnp.float32
    )
    self_branch = after_grad.astype(jnp.bfloat16)
    output_self_grad = weight_gradient(attended, self_branch)
    self_out_grad = (
        back_product(self_branch, output_self)
        .astype(jnp.bfloat16)
        .reshape(targets, key_heads, group_size, HEAD_DIM)
    )
    keys_self_grad = jnp.zeros((targets, key_heads, HEAD_DIM), jnp.float32)
    values_self_grad = jnp.zeros((targets, key_heads, HEAD_DIM), jnp.float32)
    bias_table_grad = jnp.zeros((BUCKETS, head_count), jnp.float32)
    self_query_parts = []
    for block_index in range(SLOTS):
        bias_block, allowed, pair_onehot = self_terms(block_index)
        lower = block_index * SHORT
        query_part, keys_part, values_part, scores_grad = attend_back(
            queries[lower : lower + SHORT],
            keys_self,
            values_self,
            bias_block,
            allowed,
            self_logsum[block_index],
            self_out_grad[lower : lower + SHORT],
        )
        self_query_parts.append(query_part)
        keys_self_grad = keys_self_grad + keys_part
        values_self_grad = values_self_grad + values_part
        scores_wide = scores_grad.astype(jnp.float32).reshape(head_count, SHORT, targets)
        bias_table_grad = bias_table_grad + jnp.einsum(
            "hsu,sub->bh", scores_wide, pair_onehot, precision=HIGHEST
        )
    query_grad = jnp.concatenate(self_query_parts, axis=0).reshape(targets, model_width)
    key_grad = keys_self_grad.astype(jnp.bfloat16).reshape(targets, pair_width)
    value_grad = values_self_grad.astype(jnp.bfloat16).reshape(targets, pair_width)
    query_self_grad = weight_gradient(hidden_one, query_grad)
    key_self_grad = weight_gradient(hidden_one, key_grad)
    value_self_grad = weight_gradient(hidden_one, value_grad)
    one_grad = (
        back_product(query_grad, query_self)
        + back_product(key_grad, key_self)
        + back_product(value_grad, value_self)
    )
    through_one, gain_one = norm_backward(inputs_wide, scaling_one, norm_self, one_grad)
    norm_self_grad = jnp.sum(gain_one, axis=0)
    inputs_grad = after_grad + through_one
    bias_table_grad = lax.psum(bias_table_grad, "seq")
    joined = (
        lax.psum_scatter(norm_self_grad, "seq", scatter_dimension=0, tiled=True),
        lax.psum_scatter(query_self_grad, "seq", scatter_dimension=0, tiled=True),
        lax.psum_scatter(key_self_grad, "seq", scatter_dimension=0, tiled=True),
        lax.psum_scatter(value_self_grad, "seq", scatter_dimension=0, tiled=True),
        lax.psum_scatter(output_self_grad, "seq", scatter_dimension=0, tiled=True),
        lax.psum_scatter(norm_cross_grad, "seq", scatter_dimension=0, tiled=True),
        lax.psum_scatter(query_cross_grad, "seq", scatter_dimension=0, tiled=True),
        lax.psum_scatter(output_cross_grad, "seq", scatter_dimension=0, tiled=True),
        lax.psum_scatter(norm_feed_grad, "seq", scatter_dimension=0, tiled=True),
        lax.psum_scatter(gate_proj_grad, "seq", scatter_dimension=0, tiled=True),
        lax.psum_scatter(up_proj_grad, "seq", scatter_dimension=0, tiled=True),
        lax.psum_scatter(down_proj_grad, "seq", scatter_dimension=0, tiled=True),
    )
    key_cross_grad, value_cross_grad = (
        lax.psum_scatter(key_cross_grad, ("seq", "mem"), scatter_dimension=0, tiled=True),
        lax.psum_scatter(value_cross_grad, ("seq", "mem"), scatter_dimension=0, tiled=True),
    )
    return (
        outputs,
        inputs_grad,
        memory_grad,
        joined[0],
        joined[1],
        joined[2],
        joined[3],
        joined[4],
        bias_table_grad,
        joined[5],
        joined[6],
        key_cross_grad,
        value_cross_grad,
        joined[7],
        joined[8],
        joined[9],
        joined[10],
        joined[11],
    )


def solution(mesh):
    placed = (
        P("seq", None),
        P("seq", "mem", None),
        P("seq", None),
        P("seq"),
        P("seq"),
        P(),
        P(),
        P(),
        P(),
        P(),
        P(),
        P(),
        P(),
        P(),
        P(),
        P(),
        P(),
        P(),
        P(),
        P(),
        P(),
    )
    return jax.shard_map(
        shards,
        mesh=mesh,
        in_specs=placed,
        out_specs=(
            P("seq", None),
            P("seq", None),
            P("seq", "mem", None),
            P("seq"),
            P("seq", None),
            P("seq", None),
            P("seq", None),
            P("seq", None),
            P(),
            P("seq"),
            P("seq", None),
            P(("seq", "mem"), None),
            P(("seq", "mem"), None),
            P("seq", None),
            P("seq"),
            P("seq", None),
            P("seq", None),
            P("seq", None),
        ),
        check_vma=False,
    )
```

profile of v0, /device:TPU:0, one launch (start us, length us, event | category | flops | bytes accessed | tf_op | source)
XLA Modules:
  0.0 1669.3 jit_solution(715726340128226051)
XLA Ops:
  12.9 9.9 all_gather.7
  26.8 8.2 all_gather.6
  42.8 101.4 %gather_fusion.3 = s32[16384]{0:T(1024)S(1)} fusion(s32[256]{0:T(256)S(1)} %copy-done.1, s32[16384]{0:T(1024)S(1)} %broadcast_clamp_fusion), kind=kCustom, calls=%fused_computation.3 | custom fusion | bytes 196608 | tf_op jit(solution)/shard_map/gather | solution.py:138
  145.0 101.4 %gather_fusion.2 = s32[16384]{0:T(1024)S(1)} fusion(s32[256]{0:T(256)S(1)} %copy-done.1, s32[16384]{0:T(1024)S(1)} %broadcast_clamp_fusion.1), kind=kCustom, calls=%fused_computation.2 | custom fusion | bytes 196608 | tf_op jit(solution)/shard_map/gather | solution.py:138
  247.2 101.4 %gather_fusion.1 = s32[16384]{0:T(1024)S(1)} fusion(s32[256]{0:T(256)S(1)} %copy-done.1, s32[16384]{0:T(1024)S(1)} %broadcast_clamp_fusion.2), kind=kCustom, calls=%fused_computation.1 | custom fusion | bytes 196608 | tf_op jit(solution)/shard_map/gather | solution.py:138
  349.3 101.7 %gather_fusion = s32[16384]{0:T(1024)S(1)} fusion(s32[256]{0:T(256)S(1)} %copy-done.1, s32[16384]{0:T(1024)S(1)} %broadcast_clamp_fusion.3), kind=kCustom, calls=%fused_computation | custom fusion | bytes 196608 | tf_op jit(solution)/shard_map/gather | solution.py:138
  500.3 5.1 fusion.216
  508.8 9.8 multiply_convert_fusion
  622.2 3.8 fusion.192
  632.2 3.8 fusion.140
  642.2 7.5 fusion.221
  649.7 7.4 fusion.220
  657.3 7.4 fusion.222
  675.7 59.9 %all-reduce.5 = (f32[1024]{0:T(1024)S(1)}, f32[32,16]{0,1:T(8,128)}, f32[1024]{0:T(1024)S(1)}, f32[1024]{0:T(1024)S(1)}) all-reduce(f32[1024]{0:T(1024)S(1)} %get-tuple-element.76, f32[32,16]{0,1:T(8,128)S(1)} %fusion.82, f32[1024]{0:T(1024)S(1)} %copy-done.146, ...), channel_id=2, replica_groups=mesh['seq'=16,'mem'=2] {'seq'}, use_global_device_ids=true, to_apply=%region_31.32.clone | all-reduce | flops 3584 | bytes 28672
  742.5 5.2 fusion.31
  747.7 84.5 %reduce-scatter.36.cloned.1.call-done = f32[32,512]{1,0:T(8,128)} async-done(((f32[1024,512]{1,0:T(8,128)}), f32[32,512]{1,0:T(8,128)}) %reduce-scatter.36.cloned.1.call-update) | async-done | bytes 65552
  832.2 136.4 %reduce-scatter.34.cloned.1.call-done = f32[32,512]{1,0:T(8,128)} async-done(((f32[1024,512]{1,0:T(8,128)}), f32[32,512]{1,0:T(8,128)}) %reduce-scatter.34.cloned.1.call-update) | async-done | bytes 65552
  968.5 73.3 %reduce-scatter.24.cloned.1.call-done = f32[64,1024]{1,0:T(8,128)} async-done(((f32[1024,1024]{1,0:T(8,128)}), f32[64,1024]{1,0:T(8,128)}) %reduce-scatter.24.cloned.1.call-update) | async-done | bytes 262160 | tf_op jit(solution)/shard_map/reduce_scatter | solution.py:343
  1041.8 76.3 %reduce-scatter.22.cloned.1.call-done = f32[64,1024]{1,0:T(8,128)} async-done(((f32[1024,1024]{1,0:T(8,128)}), f32[64,1024]{1,0:T(8,128)}) %reduce-scatter.22.cloned.1.call-update) | async-done | bytes 262160 | tf_op jit(solution)/shard_map/reduce_scatter | solution.py:341
  1118.1 76.2 %reduce-scatter.26.cloned.1.call-done = f32[64,1024]{1,0:T(8,128)} async-done(((f32[1024,1024]{1,0:T(8,128)}), f32[64,1024]{1,0:T(8,128)}) %reduce-scatter.26.cloned.1.call-update) | async-done | bytes 262160 | tf_op jit(solution)/shard_map/reduce_scatter | solution.py:344
  1194.3 76.4 %reduce-scatter.16.cloned.1.call-done = f32[64,1024]{1,0:T(8,128)} async-done(((f32[1024,1024]{1,0:T(8,128)}), f32[64,1024]{1,0:T(8,128)}) %reduce-scatter.16.cloned.1.call-update) | async-done | bytes 262160 | tf_op jit(solution)/shard_map/reduce_scatter | solution.py:338
  1270.6 130.1 %reduce-scatter.30.cloned.1.call-done = f32[64,2816]{1,0:T(8,128)} async-done(((f32[1024,2816]{1,0:T(8,128)}), f32[64,2816]{1,0:T(8,128)}) %reduce-scatter.30.cloned.1.call-update) | async-done | bytes 720912 | tf_op jit(solution)/shard_map/reduce_scatter | solution.py:347
  1400.7 131.1 %reduce-scatter.28.cloned.1.call-done = f32[64,2816]{1,0:T(8,128)} async-done(((f32[1024,2816]{1,0:T(8,128)}), f32[64,2816]{1,0:T(8,128)}) %reduce-scatter.28.cloned.1.call-update) | async-done | bytes 720912 | tf_op jit(solution)/shard_map/reduce_scatter | solution.py:346
  1531.9 130.7 %reduce-scatter.32.cloned.1.call-done = f32[176,1024]{1,0:T(8,128)} async-done(((f32[2816,1024]{1,0:T(8,128)}), f32[176,1024]{1,0:T(8,128)}) %reduce-scatter.32.cloned.1.call-update) | async-done | bytes 720912 | tf_op jit(solution)/shard_map/reduce_scatter | solution.py:348
  (559 shorter events, 202.7 us)
Async XLA Ops:
  7.2 473.5 %copy-start = (bf16[1024,1024]{1,0:T(8,128)(2,1)S(1)}, bf16[1024,1024]{1,0:T(8,128)(2,1)}, u32[]{:S(2)}) copy-start(bf16[1024,1024]{1,0:T(8,128)(2,1)} %param.34) | copy-start | bytes 6291460
  7.2 740.5 %reduce-scatter.20.cloned.1.call-start = ((), (), s32[]{:S(2)}) async-start(), calls=%async_computation.13 | async-start | bytes 2228224 | tf_op jit(solution)/shard_map/reduce_scatter | solution.py:340
  7.3 137.6 %copy-start.149 = (s32[64]{0:T(128)}, s32[64]{0:T(128)S(1)}, u32[]{:S(2)}) copy-start(s32[64]{0:T(128)S(1)} %iota_add_fusion.1) | copy-start | bytes 772
  7.3 35.4 %copy-start.151 = (s32[64]{0:T(128)}, s32[64]{0:T(128)S(1)}, u32[]{:S(2)}) copy-start(s32[64]{0:T(128)S(1)} %iota_add_fusion) | copy-start | bytes 772
  10.8 14.1 copy-start.38
  24.9 12.2 copy-start.13
  26.6 16.2 copy-start.1
  37.3 421.7 %copy-start.133 = (f32[256]{0:T(256)}, f32[256]{0:T(256)S(1)}, u32[]{:S(2)}) copy-start(f32[256]{0:T(256)S(1)} %add_rsqrt_fusion.2) | copy-start | bytes 3076
  349.3 102.4 %copy-start.116 = (f32[1024]{0:T(1024)S(1)}, f32[1024]{0:T(1024)}, u32[]{:S(2)}) copy-start(f32[1024]{0:T(1024)} %param.27) | copy-start | bytes 12292
  457.0 20.3 %copy-start.39 = (bf16[256,512]{0,1:T(8,128)(2,1)}, bf16[256,512]{0,1:T(8,128)(2,1)S(1)}, u32[]{:S(2)}) copy-start(bf16[256,512]{0,1:T(8,128)(2,1)S(1)} %copy.153) | copy-start | bytes 786436
  500.1 22.6 %copy-start.33 = (f32[256,1024]{1,0:T(8,128)}, f32[256,1024]{1,0:T(8,128)S(1)}, u32[]{:S(2)}) copy-start(f32[256,1024]{1,0:T(8,128)S(1)} %get-tuple-element.128) | copy-start | bytes 3145732
  505.5 14.8 slice-start.2
  565.2 182.5 %reduce-scatter.18.cloned.1.call-start = ((), (), s32[]{:S(2)}) async-start(), calls=%async_computation.12 | async-start | bytes 2228224 | tf_op jit(solution)/shard_map/reduce_scatter | solution.py:339
  577.1 255.0 %reduce-scatter.36.cloned.1.call-start = ((), (), s32[]{:S(2)}) async-start(), calls=%async_computation.21 | async-start | bytes 2162688
  604.1 364.4 %reduce-scatter.34.cloned.1.call-start = ((), (), s32[]{:S(2)}) async-start(), calls=%async_computation.20 | async-start | bytes 2162688
  621.5 420.3 %reduce-scatter.24.cloned.1.call-start = ((), (), s32[]{:S(2)}) async-start(), calls=%async_computation.15 | async-start | bytes 4456448 | tf_op jit(solution)/shard_map/reduce_scatter | solution.py:343
  626.0 492.0 %reduce-scatter.22.cloned.1.call-start = ((), (), s32[]{:S(2)}) async-start(), calls=%async_computation.14 | async-start | bytes 4456448 | tf_op jit(solution)/shard_map/reduce_scatter | solution.py:341
  631.0 563.2 %reduce-scatter.26.cloned.1.call-start = ((), (), s32[]{:S(2)}) async-start(), calls=%async_computation.16 | async-start | bytes 4456448 | tf_op jit(solution)/shard_map/reduce_scatter | solution.py:344
  636.1 634.6 %reduce-scatter.16.cloned.1.call-start = ((), (), s32[]{:S(2)}) async-start(), calls=%async_computation.11 | async-start | bytes 4456448 | tf_op jit(solution)/shard_map/reduce_scatter | solution.py:338
  642.1 758.6 %reduce-scatter.30.cloned.1.call-start = ((), (), s32[]{:S(2)}) async-start(), calls=%async_computation.18 | async-start | bytes 12255232 | tf_op jit(solution)/shard_map/reduce_scatter | solution.py:347
  649.7 882.2 %reduce-scatter.28.cloned.1.call-start = ((), (), s32[]{:S(2)}) async-start(), calls=%async_computation.17 | async-start | bytes 12255232 | tf_op jit(solution)/shard_map/reduce_scatter | solution.py:346
  657.2 1005.4 %reduce-scatter.32.cloned.1.call-start = ((), (), s32[]{:S(2)}) async-start(), calls=%async_computation.19 | async-start | bytes 12255232 | tf_op jit(solution)/shard_map/reduce_scatter | solution.py:348
  674.0 63.3 %copy-start.84 = (bf16[256,512]{1,0:T(8,128)(2,1)S(1)}, bf16[256,512]{1,0:T(8,128)(2,1)}, u32[]{:S(2)}) copy-start(bf16[256,512]{1,0:T(8,128)(2,1)} %reshape.576) | copy-start | bytes 786436
  675.7 63.4 %copy-start.91 = (bf16[256,512]{1,0:T(8,128)(2,1)S(1)}, bf16[256,512]{1,0:T(8,128)(2,1)}, u32[]{:S(2)}) copy-start(bf16[256,512]{1,0:T(8,128)(2,1)} %reshape.577) | copy-start | bytes 786436
  (153 other events, 381.5 us)
Sparse Core Ops, SparseCore 0:
  565.3 62.7 reduce-scatter.19
  632.9 60.6 reduce-scatter.17
  696.4 135.7 reduce-scatter.35
  834.9 133.5 reduce-scatter.33
  972.8 68.9 reduce-scatter.23
  1046.6 71.4 reduce-scatter.21
  1122.5 71.7 reduce-scatter.25
  1199.2 71.4 reduce-scatter.15
  1275.3 125.3 reduce-scatter.29
  1405.8 126.0 reduce-scatter.27
  1536.5 126.0 reduce-scatter.31
where the time goes:
time: 1680 us; the launch traced here: 1670 us
  waiting for transfers between devices  915 us (54%)
  local copies, waits for them, and re-layouts  490 us (29%)
  matrix products  143 us (9%)
  blocking collectives  78 us (5%)
  other arithmetic  24.3 us (1%)
  between operations  17.7 us (1%)
    gather x8, local copies, waits for them, and re-layouts, self_terms(): distance_bucket[clipped][:, :, None] == bucket_range[None, None, :]  408 us
    unnamed x13, waiting for transfers between devices  221 us
    reduce_scatter x1, waiting for transfers between devices, shards(): lax.psum_scatter(gate_proj_grad, 'seq', scatter_dimension=0, tiled=True)  131 us
    reduce_scatter x1, waiting for transfers between devices, shards(): lax.psum_scatter(down_proj_grad, 'seq', scatter_dimension=0, tiled=True)  131 us
    reduce_scatter x1, waiting for transfers between devices, shards(): lax.psum_scatter(up_proj_grad, 'seq', scatter_dimension=0, tiled=True)  130 us
    reduce_scatter x1, waiting for transfers between devices, shards(): lax.psum_scatter(query_self_grad, 'seq', scatter_dimension=0, tiled=True)  76.4 us
    reduce_scatter x1, waiting for transfers between devices, shards(): lax.psum_scatter(output_self_grad, 'seq', scatter_dimension=0, tiled=True)  76.3 us
    reduce_scatter x1, waiting for transfers between devices, shards(): lax.psum_scatter(output_cross_grad, 'seq', scatter_dimension=0, tiled=True)  76.2 us
  transfers between devices with their start and end apart: 11, of which 9 were waited for; matrix products, arithmetic and copies ran while one was open for 7% of the time, Pallas kernels for 0%

commit v1 on v0

v1 whole, which is shorter than its diff:
```python
import functools

import jax
import jax.numpy as jnp
from jax import lax
from jax.experimental import pallas as pl
from jax.experimental.pallas import tpu as pltpu
from jax.sharding import PartitionSpec as P

HEAD_DIM = 64
BUCKETS = 32
SHORT = 64
SLOTS = 4
EPSILON = 1e-06
MASKED = -1e30
TILE = 256
VMEM_LIMIT = 60 * 2**20
F32 = jnp.float32
BF16 = jnp.bfloat16
GELU_C = 0.7978845608028654
GELU_A = 0.044715


def dot_nn(left, right):
    return lax.dot_general(left, right, (((1,), (0,)), ((), ())), preferred_element_type=F32)


def dot_nt(left, right):
    return lax.dot_general(left, right, (((1,), (1,)), ((), ())), preferred_element_type=F32)


def dot_tn(left, right):
    return lax.dot_general(left, right, (((0,), (0,)), ((), ())), preferred_element_type=F32)


def scaling_of(values):
    return lax.rsqrt(jnp.mean(values * values, axis=-1, keepdims=True) + EPSILON)


def norm_back(values, gain, upstream):
    scaling = scaling_of(values)
    normed = values * scaling
    scaled = upstream * gain
    through = scaling * (scaled - normed * jnp.mean(scaled * normed, axis=-1, keepdims=True))
    return through, jnp.sum(upstream * normed, axis=0, keepdims=True)


def tiles(count, body):
    @pl.loop(0, count)
    def _(j):
        body(pl.ds(pl.multiple_of(j * TILE, TILE), TILE))


def start_all(sources, targets, sems):
    copies = [
        pltpu.make_async_copy(source, target, sems.at[i])
        for i, (source, target) in enumerate(zip(sources, targets, strict=True))
    ]
    for copy in copies:
        copy.start()
    return copies


def two_rows(pair):
    return jnp.concatenate([pair[:, :HEAD_DIM], pair[:, HEAD_DIM:]], axis=0)


def two_columns(stack):
    rows = stack.shape[0] // 2
    return jnp.concatenate([stack[:rows], stack[rows:]], axis=1)


def self_forward(
    long_ref, x_ref, gain_ref, bias_ref, wq_hbm, wk_hbm, wv_hbm, wo_hbm,
    h_ref, q_ref, k_ref, v_ref, att_ref, p_ref, out_ref,
    wq, wk, wv, wo, sems,
):
    copies = start_all((wq_hbm, wk_hbm, wv_hbm, wo_hbm), (wq, wk, wv, wo), sems)
    rows, width = x_ref.shape
    is_long = long_ref[0] == 1
    x = x_ref[...].astype(F32)
    h_ref[...] = (x * scaling_of(x) * gain_ref[...]).astype(BF16)
    for copy, weight, result in zip(copies, (wq, wk, wv), (q_ref, k_ref, v_ref)):
        copy.wait()

        def project(columns, weight=weight, result=result):
            result[:, columns] = dot_nn(h_ref[...], weight[:, columns]).astype(BF16)

        tiles(weight.shape[1] // TILE, project)

    t = lax.broadcasted_iota(jnp.int32, (rows, rows), 0)
    u = lax.broadcasted_iota(jnp.int32, (rows, rows), 1)
    allowed = (u <= t) & (is_long | (t // SHORT == u // SHORT))

    @pl.loop(0, k_ref.shape[1] // 128)
    def _(pair):
        k_pair = k_ref[:, pl.ds(pl.multiple_of(pair * 128, 128), 128)]
        v_pair = v_ref[:, pl.ds(pl.multiple_of(pair * 128, 128), 128)]
        for i in range(2):
            lanes = slice(i * HEAD_DIM, (i + 1) * HEAD_DIM)
            columns = pl.ds(pl.multiple_of(pair * 256 + i * 128, 128), 128)
            q_pair = q_ref[:, columns]
            parts = []
            for h in range(2):
                head = pair * 4 + i * 2 + h
                scores = dot_nt(q_pair[:, h * HEAD_DIM : (h + 1) * HEAD_DIM], k_pair[:, lanes])
                bias = jnp.broadcast_to(bias_ref[pl.ds(head, 1), :], (rows, rows))
                scores += pltpu.roll(bias, 0, 1, stride=1, stride_axis=0)
                scores = jnp.where(allowed, scores, MASKED)
                weights = jnp.exp(scores - jnp.max(scores, axis=-1, keepdims=True))
                weights = weights / jnp.sum(weights, axis=-1, keepdims=True)
                p_ref[pair * 2 + i, h * rows : (h + 1) * rows, :] = weights
                parts.append(dot_nn(weights.astype(BF16), v_pair[:, lanes]))
            att_ref[:, columns] = jnp.concatenate(parts, axis=1).astype(BF16)

    copies[3].wait()

    def leave(columns):
        out_ref[:, columns] = x_ref[:, columns].astype(F32) + dot_nn(att_ref[...], wo[:, columns])

    tiles(width // TILE, leave)


def cross_and_feed(
    long_ref, len_ref, x_ref, cot_ref, own_ref, other_ref, gain_ref, feed_gain_ref,
    wq_hbm, wo_hbm, gate_hbm, up_hbm, down_hbm,
    out_ref, grad_ref, feed_gain_grad_ref, h_ref, q_ref, att_ref, p_ref, chosen_ref,
    feed_ref, act_ref, gate_grad_ref, up_grad_ref,
    wq, wo, gate, up, down, acc, three, sems, feed_sems,
):
    copies = start_all((wq_hbm, wo_hbm), (wq, wo), sems)
    rows, width = x_ref.shape
    hidden = gate.shape[1]

    def feed_copies(j):
        columns = pl.ds(pl.multiple_of(j * TILE, TILE), TILE)
        return (
            pltpu.make_async_copy(gate_hbm.at[:, columns], gate.at[:, columns], feed_sems.at[0, j]),
            pltpu.make_async_copy(up_hbm.at[:, columns], up.at[:, columns], feed_sems.at[1, j]),
            pltpu.make_async_copy(down_hbm.at[columns, :], down.at[columns, :], feed_sems.at[2, j]),
        )

    @pl.loop(0, hidden // TILE)
    def _(j):
        for copy in feed_copies(j):
            copy.start()

    is_long = long_ref[0] == 1
    x = x_ref[...]
    h_ref[...] = (x * scaling_of(x) * gain_ref[...]).astype(BF16)

    me = lax.axis_index("mem")
    span = own_ref.shape[1]
    for part, ref in ((me, own_ref), (1 - me, other_ref)):
        positions = pl.ds(pl.multiple_of(part * span, span), span)
        for b in range(SLOTS):
            chosen_ref[b, positions, :] = jnp.where(is_long, ref[0], ref[b])

    copies[0].wait()

    def project(columns):
        q_ref[:, columns] = dot_nn(h_ref[...], wq[:, columns]).astype(BF16)

    tiles(width // TILE, project)
    slot_width = chosen_ref.shape[1]
    half = chosen_ref.shape[2] // 2
    positions = lax.broadcasted_iota(jnp.int32, (2 * SHORT, slot_width), 1)

    @pl.loop(0, half // 128)
    def _(pair):
        for i in range(2):
            columns = pl.ds(pl.multiple_of(pair * 256 + i * 128, 128), 128)
            lanes = slice(i * HEAD_DIM, (i + 1) * HEAD_DIM)
            for b in range(SLOTS):
                block = slice(b * SHORT, (b + 1) * SHORT)
                keys = chosen_ref[b, :, pl.ds(pl.multiple_of(pair * 128, 128), 128)][:, lanes]
                values = chosen_ref[b, :, pl.ds(pl.multiple_of(half + pair * 128, 128), 128)][:, lanes]
                length = jnp.where(is_long, len_ref[0], len_ref[b])
                scores = dot_nt(two_rows(q_ref[block, columns]), keys)
                scores = jnp.where(positions < length, scores, MASKED)
                weights = jnp.exp(scores - jnp.max(scores, axis=-1, keepdims=True))
                weights = weights / jnp.sum(weights, axis=-1, keepdims=True)
                p_ref[pair * 2 + i, b] = weights
                att_ref[block, columns] = two_columns(dot_nn(weights.astype(BF16), values)).astype(BF16)

    copies[1].wait()

    def leave(columns):
        acc[:, columns] = x_ref[:, columns] + dot_nn(att_ref[...], wo[:, columns])

    tiles(width // TILE, leave)
    x = acc[...]
    feed_ref[...] = (x * scaling_of(x) * feed_gain_ref[...]).astype(BF16)
    grad_ref[...] = x
    three[...] = jnp.zeros_like(three)

    @pl.loop(0, hidden // TILE)
    def _(j):
        for copy in feed_copies(j):
            copy.wait()
        columns = pl.ds(pl.multiple_of(j * TILE, TILE), TILE)
        g = dot_nn(feed_ref[...], gate[:, columns])
        u = dot_nn(feed_ref[...], up[:, columns])
        square = g * g
        tanh = jnp.tanh(GELU_C * (g + GELU_A * g * square))
        gelu = 0.5 * g * (1.0 + tanh)
        act = (gelu * u).astype(BF16)
        act_ref[:, columns] = act
        acc[...] += dot_nn(act, down[columns, :])
        act_grad = dot_nt(cot_ref[...], down[columns, :])
        slope = 0.5 * (1.0 + tanh) + 0.5 * g * (1.0 - tanh * tanh) * (
            GELU_C * (1.0 + 3.0 * GELU_A * square)
        )
        gate_grad = (act_grad * u * slope).astype(BF16)
        up_grad = (act_grad * gelu).astype(BF16)
        gate_grad_ref[:, columns] = gate_grad
        up_grad_ref[:, columns] = up_grad
        three[...] += dot_nt(gate_grad, gate[:, columns]) + dot_nt(up_grad, up[:, columns])

    out_ref[...] = acc[...].astype(BF16)
    through, gain_grad = norm_back(grad_ref[...], feed_gain_ref[...], three[...])
    feed_gain_grad_ref[...] = gain_grad
    grad_ref[...] = cot_ref[...].astype(F32) + through


def diagonal_sums(scores):
    rows, width = scores.shape
    while rows > 8:
        rows //= 2
        scores = scores[:rows] + pltpu.roll(scores[rows:], width - rows, 1)
    t = lax.broadcasted_iota(jnp.int32, scores.shape, 0)
    for bit in (4, 2, 1):
        scores = jnp.where((t & bit) != 0, pltpu.roll(scores, width - bit, 1), scores)
    return jnp.sum(scores, axis=0, keepdims=True)


def attention_back(weights, values, keys, queries, out_grad):
    values_grad = dot_tn(weights.astype(BF16), out_grad)
    weights_grad = dot_nt(out_grad, values)
    inner = jnp.sum(weights * weights_grad, axis=-1, keepdims=True)
    scores_grad = (weights * (weights_grad - inner)).astype(BF16)
    queries_grad = dot_nn(scores_grad, keys)
    keys_grad = dot_tn(scores_grad, queries)
    return queries_grad, keys_grad, values_grad, scores_grad


def gradient_into(result, left_ref, right_ref, columns):
    @pl.loop(0, left_ref.shape[1] // TILE)
    def _(j):
        rows = pl.ds(pl.multiple_of(j * TILE, TILE), TILE)
        result[rows, :] = dot_tn(left_ref[:, rows], right_ref[:, columns]).astype(result.dtype)


def backward(
    long_ref, x_ref, mid_ref, grad_ref, cot_ref, gain_one_ref, gain_two_ref,
    h1_ref, q_ref, k_ref, v_ref, att_ref, p_ref,
    h2_ref, cq_ref, catt_ref, cp_ref, chosen_ref, memory_ref,
    h3_ref, act_ref, gate_grad_ref, up_grad_ref,
    wq_hbm, wk_hbm, wv_hbm, wo_hbm, wcq_hbm, wck_hbm, wcv_hbm, wco_hbm,
    in_grad_ref, mem_grad_ref, diagonal_ref, gain_grad_ref,
    g_q, g_k, g_v, g_o, g_cq, g_co, g_gate, g_up, g_down, g_ck, g_cv,
    wq, wk, wv, wo, wcq, wck, wcv, wco,
    branch, out_grad, q_grad, k_grad, v_grad, mem_k, mem_v, wide, after, sems,
):
    hbm = (wco_hbm, wcq_hbm, wck_hbm, wcv_hbm, wo_hbm, wq_hbm, wk_hbm, wv_hbm)
    copies = start_all(hbm, (wco, wcq, wck, wcv, wo, wq, wk, wv), sems)
    rows, width = x_ref.shape
    half_pair = k_ref.shape[1] // 2
    half = width // 2
    half_hidden = act_ref.shape[1] // 2
    me = lax.axis_index("mem")
    is_long = long_ref[0] == 1

    def mine(size):
        return pl.ds(pl.multiple_of(me * size, 128), size)

    gradient_into(g_gate, h3_ref, gate_grad_ref, mine(half_hidden))
    gradient_into(g_up, h3_ref, up_grad_ref, mine(half_hidden))
    gradient_into(g_down, act_ref, cot_ref, mine(half))

    branch[...] = grad_ref[...].astype(BF16)
    gradient_into(g_co, catt_ref, branch, mine(half))
    copies[0].wait()

    def out_of_cross(columns):
        out_grad[:, columns] = dot_nt(branch[...], wco[columns, :]).astype(BF16)

    tiles(width // TILE, out_of_cross)
    slot_width = chosen_ref.shape[1]
    pair_width = k_ref.shape[1]

    @pl.loop(0, pair_width // 128)
    def _(pair):
        keys_at = pl.ds(pl.multiple_of(pair * 128, 128), 128)
        values_at = pl.ds(pl.multiple_of(pair_width + pair * 128, 128), 128)
        for b in range(SLOTS):
            block = slice(b * SHORT, (b + 1) * SHORT)
            keys_parts, values_parts = [], []
            for i in range(2):
                columns = pl.ds(pl.multiple_of(pair * 256 + i * 128, 128), 128)
                lanes = slice(i * HEAD_DIM, (i + 1) * HEAD_DIM)
                queries_part, keys_part, values_part, _ = attention_back(
                    cp_ref[pair * 2 + i, b],
                    chosen_ref[b, :, values_at][:, lanes],
                    chosen_ref[b, :, keys_at][:, lanes],
                    two_rows(cq_ref[block, columns]),
                    two_rows(out_grad[block, columns]),
                )
                q_grad[block, columns] = two_columns(queries_part).astype(BF16)
                keys_parts.append(keys_part)
                values_parts.append(values_part)
            mem_k[b, :, keys_at] = jnp.concatenate(keys_parts, axis=1)
            mem_v[b, :, keys_at] = jnp.concatenate(values_parts, axis=1)

    span = slot_width // 2
    positions = pl.ds(pl.multiple_of(me * span, span), span)
    for stack, result in ((mem_k, k_grad), (mem_v, v_grad)):
        total = stack[0, positions, :]
        for b in range(1, SLOTS):
            own = stack[b, positions, :]
            total += jnp.where(is_long, own, 0.0)
            result[b * span : (b + 1) * span, :] = jnp.where(is_long, 0.0, own).astype(BF16)
        result[0:span, :] = total.astype(BF16)
    gradient_into(g_ck, memory_ref, k_grad, slice(None))
    gradient_into(g_cv, memory_ref, v_grad, slice(None))
    gradient_into(g_cq, h2_ref, q_grad, mine(half))
    copies[1].wait()
    copies[2].wait()
    copies[3].wait()

    def into_cross(columns):
        mem_grad_ref[:, columns] = dot_nt(k_grad[...], wck[columns, :]) + dot_nt(
            v_grad[...], wcv[columns, :]
        )
        wide[:, columns] = dot_nt(q_grad[...], wcq[columns, :])

    tiles(width // TILE, into_cross)
    through, gain_grad = norm_back(mid_ref[...], gain_two_ref[...], wide[...])
    gain_grad_ref[1:2, :] = gain_grad
    after[...] = grad_ref[...] + through

    branch[...] = after[...].astype(BF16)
    gradient_into(g_o, att_ref, branch, mine(half))
    copies[4].wait()

    def out_of_self(columns):
        out_grad[:, columns] = dot_nt(branch[...], wo[columns, :]).astype(BF16)

    tiles(width // TILE, out_of_self)

    @pl.loop(0, pair_width // 128)
    def _(pair):
        at = pl.ds(pl.multiple_of(pair * 128, 128), 128)
        k_pair = k_ref[:, at]
        v_pair = v_ref[:, at]
        keys_parts, values_parts = [], []
        for i in range(2):
            columns = pl.ds(pl.multiple_of(pair * 256 + i * 128, 128), 128)
            lanes = slice(i * HEAD_DIM, (i + 1) * HEAD_DIM)
            queries_part, keys_part, values_part, scores_grad = attention_back(
                p_ref[pair * 2 + i],
                v_pair[:, lanes],
                k_pair[:, lanes],
                two_rows(q_ref[:, columns]),
                two_rows(out_grad[:, columns]),
            )
            q_grad[:, columns] = two_columns(queries_part).astype(BF16)
            keys_parts.append(keys_part)
            values_parts.append(values_part)
            for h in range(2):
                diagonal_ref[pl.ds(pair * 4 + i * 2 + h, 1), :] = diagonal_sums(
                    scores_grad[h * rows : (h + 1) * rows].astype(F32)
                )
        k_grad[:, at] = jnp.concatenate(keys_parts, axis=1).astype(BF16)
        v_grad[:, at] = jnp.concatenate(values_parts, axis=1).astype(BF16)

    gradient_into(g_q, h1_ref, q_grad, mine(half))
    gradient_into(g_k, h1_ref, k_grad, mine(half_pair))
    gradient_into(g_v, h1_ref, v_grad, mine(half_pair))
    for copy in copies[5:]:
        copy.wait()

    def into_self(columns):
        wide[:, columns] = (
            dot_nt(q_grad[...], wq[columns, :])
            + dot_nt(k_grad[...], wk[columns, :])
            + dot_nt(v_grad[...], wv[columns, :])
        )

    tiles(width // TILE, into_self)
    through, gain_grad = norm_back(x_ref[...].astype(F32), gain_one_ref[...], wide[...])
    gain_grad_ref[0:1, :] = gain_grad
    in_grad_ref[...] = after[...] + through


SMEM = pl.BlockSpec(memory_space=pltpu.SMEM)
VMEM = pl.BlockSpec(memory_space=pltpu.VMEM)
ANY = pl.BlockSpec(memory_space=pl.ANY)


def shape_of(shape, dtype):
    return jax.ShapeDtypeStruct(shape, dtype)


def scratch_like(*arrays):
    return [pltpu.VMEM(array.shape, array.dtype) for array in arrays]


def call(kernel, in_specs, outs, scratch, **params):
    return pl.pallas_call(
        kernel,
        in_specs=in_specs,
        out_specs=[VMEM] * len(outs),
        out_shape=[shape_of(*out) for out in outs],
        scratch_shapes=scratch,
        compiler_params=pltpu.CompilerParams(vmem_limit_bytes=VMEM_LIMIT, **params),
    )


def shards(
    seq_size,
    inputs,
    memory,
    cotangent,
    is_long,
    memory_len,
    distance_bucket,
    norm_self,
    query_self,
    key_self,
    value_self,
    output_self,
    bias_table,
    norm_cross,
    query_cross,
    key_cross,
    value_cross,
    output_cross,
    norm_feed,
    gate_proj,
    up_proj,
    down_proj,
):
    rows, width = inputs.shape
    pair_width = key_self.shape[1]
    hidden = gate_proj.shape[1]
    key_heads = pair_width // HEAD_DIM
    head_count = width // HEAD_DIM
    span = memory.shape[1]
    gain_one, gain_two, gain_three = (g.reshape(1, width) for g in (norm_self, norm_cross, norm_feed))
    memory_rows = memory.reshape(-1, width)
    own_pairs = jnp.concatenate(
        [
            jnp.dot(memory_rows, weight, preferred_element_type=F32).astype(BF16)
            for weight in (key_cross, value_cross)
        ],
        axis=1,
    ).reshape(SLOTS, span, 2 * pair_width)
    other_pairs = lax.ppermute(own_pairs, "mem", [(0, 1), (1, 0)])

    backwards = jnp.roll(distance_bucket[::-1], 1)
    onehot = backwards[None, :] == jnp.arange(BUCKETS)[:, None]
    bias_rows = jnp.sum(jnp.where(onehot[None], bias_table.T[:, :, None], 0.0), axis=1)

    act = ((rows, width), BF16)
    pair = ((rows, pair_width), BF16)
    wide = ((rows, width), F32)
    line = ((1, width), F32)
    broad = ((rows, hidden), BF16)
    h1, q, k, v, att, p, after_self = call(
        self_forward,
        [SMEM] + [VMEM] * 3 + [ANY] * 4,
        [act, act, pair, pair, act, ((key_heads, 2 * rows, rows), F32), wide],
        scratch_like(query_self, key_self, value_self, output_self) + [pltpu.SemaphoreType.DMA((4,))],
    )(is_long, inputs, gain_one, bias_rows, query_self, key_self, value_self, output_self)

    outputs, cross_grad, feed_gain_grad, h2, cq, catt, cp, chosen, h3, activated, gate_grad, up_grad = call(
        cross_and_feed,
        [SMEM] * 2 + [VMEM] * 6 + [ANY] * 5,
        [
            act, wide, line, act, act, act,
            ((key_heads, SLOTS, 2 * SHORT, 2 * span), F32),
            ((SLOTS, 2 * span, 2 * pair_width), BF16),
            act, broad, broad, broad,
        ],
        scratch_like(query_cross, output_cross, gate_proj, up_proj, down_proj)
        + [pltpu.VMEM(*wide), pltpu.VMEM(*wide)]
        + [pltpu.SemaphoreType.DMA((2,)), pltpu.SemaphoreType.DMA((3, hidden // TILE))],
    )(
        is_long, memory_len, after_self, cotangent, own_pairs, other_pairs, gain_two, gain_three,
        query_cross, output_cross, gate_proj, up_proj, down_proj,
    )

    weights = (query_self, key_self, value_self, output_self, query_cross, key_cross, value_cross, output_cross)
    half = ((width, width // 2), BF16)
    half_pair = ((width, pair_width // 2), BF16)
    half_broad = ((width, hidden // 2), BF16)
    full_pair = ((width, pair_width), BF16)
    inputs_grad, memory_grad, diagonals, gain_grads, *grads = call(
        backward,
        [SMEM] + [VMEM] * 22 + [ANY] * 8,
        [
            wide, ((memory_rows.shape[0], width), F32), ((head_count, rows), F32), ((2, width), F32),
            half, half_pair, half_pair, half, half, half, half_broad, half_broad,
            ((hidden, width // 2), BF16), full_pair, full_pair,
        ],
        scratch_like(*weights)
        + [pltpu.VMEM(*act), pltpu.VMEM(*act), pltpu.VMEM(*act), pltpu.VMEM(*pair), pltpu.VMEM(*pair)]
        + [pltpu.VMEM((SLOTS, 2 * span, pair_width), F32)] * 2
        + [pltpu.VMEM(*wide), pltpu.VMEM(*wide), pltpu.SemaphoreType.DMA((8,))],
    )(
        is_long, inputs, after_self, cross_grad, cotangent, gain_one, gain_two,
        h1, q, k, v, att, p, h2, cq, catt, cp, chosen, memory_rows, h3, activated, gate_grad, up_grad,
        *weights,
    )

    small = lax.psum(
        jnp.concatenate(
            [diagonals.reshape(-1, 128), gain_grads.reshape(-1, 128), feed_gain_grad.reshape(-1, 128)]
        ),
        "seq",
    )
    size = width // seq_size
    split = diagonals.size // 128
    gains = lax.dynamic_slice_in_dim(
        small[split:].reshape(3, width), lax.axis_index("seq") * size, size, 1
    )
    bias_table_grad = jnp.einsum(
        "hj,bj->bh", small[:split].reshape(diagonals.shape), onehot.astype(F32), precision=lax.Precision.HIGHEST
    )

    def scattered(grad, axes):
        return lax.psum_scatter(grad.astype(F32), axes, scatter_dimension=0, tiled=True)

    joined = [
        lax.all_gather(scattered(grad, "seq"), "mem", axis=1, tiled=True) for grad in grads[:9]
    ]
    q_g, k_g, v_g, o_g, cq_g, co_g, gate_g, up_g, down_g = joined
    ck_g, cv_g = (scattered(grad, ("seq", "mem")) for grad in grads[9:])
    return (
        outputs,
        inputs_grad,
        memory_grad.reshape(memory.shape),
        gains[0],
        q_g,
        k_g,
        v_g,
        o_g,
        bias_table_grad,
        gains[1],
        cq_g,
        ck_g,
        cv_g,
        co_g,
        gains[2],
        gate_g,
        up_g,
        down_g,
    )


def solution(mesh):
    rows = P("seq", None)
    return jax.shard_map(
        functools.partial(shards, mesh.shape["seq"]),
        mesh=mesh,
        in_specs=(rows, P("seq", "mem", None), rows, P("seq"), P("seq")) + (P(),) * 16,
        out_specs=(rows, rows, P("seq", "mem", None), P("seq"))
        + (rows,) * 4
        + (P(), P("seq"), rows)
        + (P(("seq", "mem"), None),) * 2
        + (rows, P("seq"), rows, rows, rows),
        check_vma=False,
    )
```

time: 1680 us -> 1050 us (0.62)
  local copies, waits for them, and re-layouts: 490 us -> 14 us
  waiting for transfers between devices: 915 us -> 749 us
  matrix products: 143 us -> 4.39 us
  Pallas kernels: 0 us -> 106 us
  blocking collectives: 78 us -> 127 us
    gather x8 -> x0, local copies, waits for them, and re-layouts: 408 us -> none  [self_terms(): distance_bucket[clipped][:, :, None] == bucket_range[None, None, :]]
    unnamed x13 -> x11, waiting for transfers between devices: 221 us -> 0.18 us
    dot_general x89 -> x3, matrix products: 143 us -> 4.39 us  [the longest x2 3.65 us: shards(): jnp.dot(memory_rows, weight, preferred_element_type=F32).astype(BF16)]
    pallas_call x0 -> x3, Pallas kernels: none -> 106 us  [the longest x1 52.2 us: shards(): call(backward, [SMEM] + [VMEM] * 22 + [ANY] * 8, [wide, ((memory_rows.sha...]
    psum x0 -> x1, blocking collectives: none -> 61.2 us  [shards(): lax.psum(jnp.concatenate([diagonals.reshape(-1, 128), gain_grads.reshape(...]
    unnamed x1 -> x0, blocking collectives: 59.9 us -> none
    reduce_scatter x9 -> x11, waiting for transfers between devices: 694 us -> 749 us  [scattered(): lax.psum_scatter(grad.astype(F32), axes, scatter_dimension=0, tiled=True)]
    all_gather x2 -> x9, blocking collectives: 18.1 us -> 65.9 us  [shards(): lax.all_gather(scattered(grad, 'seq'), 'mem', axis=1, tiled=True)]
  transfers between devices with their start and end apart: 11 -> 12, of which waited for: 9 -> 10; matrix products, arithmetic and copies ran while one was open for 7% -> 2% of each run, Pallas kernels for 0% -> 1%
where the time goes in v1:
time: 1050 us; the launch traced here: 1040 us
  waiting for transfers between devices  749 us (71%)
  blocking collectives  127 us (12%)
  Pallas kernels  106 us (10%)
  other arithmetic  25.1 us (2%)
  between operations  14.8 us (1%)
  local copies, waits for them, and re-layouts  14 us (1%)
    reduce_scatter x11, waiting for transfers between devices, scattered(): lax.psum_scatter(grad.astype(F32), axes, scatter_dimension=0, tiled=True)  749 us
    all_gather x9, blocking collectives, shards(): lax.all_gather(scattered(grad, 'seq'), 'mem', axis=1, tiled=True)  65.9 us
    psum x1, blocking collectives, shards(): lax.psum(jnp.concatenate([diagonals.reshape(-1, 128), gain_grads.reshape(...  61.2 us
    pallas_call x1, Pallas kernels, shards(): call(backward, [SMEM] + [VMEM] * 22 + [ANY] * 8, [wide, ((memory_rows.sha...  52.2 us
    pallas_call x1, Pallas kernels, shards(): call(cross_and_feed, [SMEM] * 2 + [VMEM] * 6 + [ANY] * 5, [act, wide, lin...  38.5 us
    convert_element_type x11, other arithmetic, scattered(): grad.astype(F32)  23.6 us
  transfers between devices with their start and end apart: 12, of which 10 were waited for; matrix products, arithmetic and copies ran while one was open for 2% of the time, Pallas kernels for 1%

profile of v1, /device:TPU:0, one launch (start us, length us, event | category | flops | bytes accessed | tf_op | source)
XLA Modules:
  0.0 1044.5 jit_solution(6619121041465067013)
XLA Ops:
  17.0 15.4 %shard_map.340 = (bf16[256,1024]{1,0:T(8,128)(2,1)}, bf16[256,1024]{1,0:T(8,128)(2,1)}, bf16[256,512]{1,0:T(8,128)(2,1)}, bf16[256,512]{1,0:T(8,128)(2,1)}, bf16...) custom-call(s32[1]{0:T(128)S(6)} %copy.48.long_ref, bf16[256,1024]{1,0:T(8,128)(2,1)} %x_ref.3, ...), custom_call_target="tpu_custom_call" | custom-call | tf_op jit(solution)/shard_map/pallas_call | solution.py:470
  33.2 38.5 %shard_map.341 = (bf16[256,1024]{1,0:T(8,128)(2,1)}, f32[256,1024]{1,0:T(8,128)}, f32[1,1024]{1,0:T(1,128)}, bf16[256,1024]{1,0:T(8,128)(2,1)}, bf16[256,1024]{1...) custom-call(s32[1]{0:T(128)S(6)} %copy.48.long_ref, ...), custom_call_target="tpu_custom_call" | custom-call | tf_op jit(solution)/shard_map/pallas_call | solution.py:477
  71.7 52.2 %shard_map.342 = (f32[256,1024]{1,0:T(8,128)}, f32[256,1024]{1,0:T(8,128)}, f32[16,256]{1,0:T(8,128)}, f32[2,1024]{1,0:T(2,128)}, bf16[1024,512]{1,0:T(8,128)(2,...) custom-call(s32[1]{0:T(128)S(6)} %copy.48.long_ref, ...), custom_call_target="tpu_custom_call" | custom-call | tf_op jit(solution)/shard_map/pallas_call | solution.py:499
  145.5 3.3 convert_element_type.52
  153.5 61.2 %psum.7 = f32[56,128]{1,0:T(8,128)S(1)} all-reduce(f32[56,128]{1,0:T(8,128)S(1)} %pad_maximum_fusion.1), channel_id=1, replica_groups=mesh['seq'=16,'mem'=2] {'seq'}, use_global_device_ids=true, to_apply=%region_1.2 | all-reduce | flops 7168 | bytes 57344 | tf_op jit(solution)/shard_map/psum | solution.py:517
  216.1 5.1 all_gather.28
  221.3 23.3 %reduce-scatter.16.cloned.1.call-done = f32[64,256]{1,0:T(8,128)} async-done(((f32[1024,256]{1,0:T(8,128)}), f32[64,256]{1,0:T(8,128)}) %reduce-scatter.16.cloned.1.call-update) | async-done | bytes 65552 | tf_op jit(solution)/shard_map/reduce_scatter | solution.py:533
  244.6 5.1 all_gather.29
  249.8 59.2 %reduce-scatter.12.cloned.1.call-done = f32[64,512]{1,0:T(8,128)} async-done(((f32[1024,512]{1,0:T(8,128)}), f32[64,512]{1,0:T(8,128)}) %reduce-scatter.12.cloned.1.call-update) | async-done | bytes 131088 | tf_op jit(solution)/shard_map/reduce_scatter | solution.py:533
  309.0 5.8 all_gather.27
  314.8 58.8 %reduce-scatter.18.cloned.1.call-done = f32[64,512]{1,0:T(8,128)} async-done(((f32[1024,512]{1,0:T(8,128)}), f32[64,512]{1,0:T(8,128)}) %reduce-scatter.18.cloned.1.call-update) | async-done | bytes 131088 | tf_op jit(solution)/shard_map/reduce_scatter | solution.py:533
  373.6 5.8 all_gather.30
  379.5 58.4 %reduce-scatter.20.cloned.1.call-done = f32[64,512]{1,0:T(8,128)} async-done(((f32[1024,512]{1,0:T(8,128)}), f32[64,512]{1,0:T(8,128)}) %reduce-scatter.20.cloned.1.call-update) | async-done | bytes 131088 | tf_op jit(solution)/shard_map/reduce_scatter | solution.py:533
  437.8 5.8 all_gather.31
  443.7 58.8 %reduce-scatter.26.cloned.1.call-done = f32[64,512]{1,0:T(8,128)} async-done(((f32[1024,512]{1,0:T(8,128)}), f32[64,512]{1,0:T(8,128)}) %reduce-scatter.26.cloned.1.call-update) | async-done | bytes 131088 | tf_op jit(solution)/shard_map/reduce_scatter | solution.py:533
  502.5 5.8 all_gather.32
  508.4 78.6 %reduce-scatter.28.cloned.1.call-done = f32[64,1408]{1,0:T(8,128)} async-done(((f32[1024,1408]{1,0:T(8,128)}), f32[64,1408]{1,0:T(8,128)}) %reduce-scatter.28.cloned.1.call-update) | async-done | bytes 360464 | tf_op jit(solution)/shard_map/reduce_scatter | solution.py:533
  587.0 10.4 all_gather.33
  597.4 74.2 %reduce-scatter.30.cloned.1.call-done = f32[64,1408]{1,0:T(8,128)} async-done(((f32[1024,1408]{1,0:T(8,128)}), f32[64,1408]{1,0:T(8,128)}) %reduce-scatter.30.cloned.1.call-update) | async-done | bytes 360464 | tf_op jit(solution)/shard_map/reduce_scatter | solution.py:533
  671.7 10.4 all_gather.34
  682.1 74.2 %reduce-scatter.32.cloned.1.call-done = f32[176,512]{1,0:T(8,128)} async-done(((f32[2816,512]{1,0:T(8,128)}), f32[176,512]{1,0:T(8,128)}) %reduce-scatter.32.cloned.1.call-update) | async-done | bytes 360464 | tf_op jit(solution)/shard_map/reduce_scatter | solution.py:533
  756.3 11.4 %all_gather.35 = f32[176,1024]{1,0:T(8,128)S(1)} all-gather(f32[176,512]{1,0:T(8,128)} %reduce-scatter.32.cloned.1.call-done), channel_id=1, replica_groups=mesh['seq'=16,'mem'=2] {'mem'}, dimensions={1}, use_global_device_ids=true | all-gather | bytes 1081344 | tf_op jit(solution)/shard_map/all_gather | solution.py:536
  767.7 127.2 %reduce-scatter.22.cloned.1.call-done = f32[32,512]{1,0:T(8,128)} async-done(((f32[1024,512]{1,0:T(8,128)}), f32[32,512]{1,0:T(8,128)}) %reduce-scatter.22.cloned.1.call-update) | async-done | bytes 65552 | tf_op jit(solution)/shard_map/reduce_scatter | solution.py:533
  894.9 136.4 %reduce-scatter.24.cloned.1.call-done = f32[32,512]{1,0:T(8,128)} async-done(((f32[1024,512]{1,0:T(8,128)}), f32[32,512]{1,0:T(8,128)}) %reduce-scatter.24.cloned.1.call-update) | async-done | bytes 65552 | tf_op jit(solution)/shard_map/reduce_scatter | solution.py:533
  (96 shorter events, 43.9 us)
Async XLA Ops:
  7.2 209.0 %reduce-scatter.14.cloned.1.call-start = ((), (), s32[]{:S(2)}) async-start(), calls=%async_computation.12 | async-start | bytes 1114112 | tf_op jit(solution)/shard_map/reduce_scatter | solution.py:533
  7.2 6.8 copy-start.15
  7.2 8.9 copy-start.13
  11.0 21.4 %copy-start.3 = (bf16[256,1024]{1,0:T(8,128)(2,1)}, bf16[256,1024]{1,0:T(8,128)(2,1)S(1)}, u32[]{:S(2)}) copy-start(bf16[256,1024]{1,0:T(8,128)(2,1)S(1)} %pad_maximum_fusion) | copy-start | bytes 1572868
  11.0 21.4 %collective-permute-start = (bf16[4,64,1024]{2,1,0:T(8,128)(2,1)S(1)}, bf16[4,64,1024]{2,1,0:T(8,128)(2,1)S(1)}, u32[]{:S(2)}, u32[]{:S(2)}) collective-permute-start(bf16[4,64,1024]{2,1,0:T(8,128)(2,1)S(1)} %bitcast.23), channel_id=1, source_target_pairs={{0,1},{1,0},{2,3},{3,2},{4,5},{5,4},{6,7},{7,6},{8,9},{9,8},{10,11... | collective-permute-start | bytes 1572872 | tf_op jit(solution)/shard_map/ppermute | solution.py:459
  123.9 2.2 copy-start.9
  126.1 118.5 %reduce-scatter.16.cloned.1.call-start = ((), (), s32[]{:S(2)}) async-start(), calls=%async_computation.13 | async-start | bytes 1114112 | tf_op jit(solution)/shard_map/reduce_scatter | solution.py:533
  127.2 181.7 %reduce-scatter.12.cloned.1.call-start = ((), (), s32[]{:S(2)}) async-start(), calls=%async_computation.11 | async-start | bytes 2228224 | tf_op jit(solution)/shard_map/reduce_scatter | solution.py:533
  127.6 1.7 copy-start.7
  129.3 244.3 %reduce-scatter.18.cloned.1.call-start = ((), (), s32[]{:S(2)}) async-start(), calls=%async_computation.14 | async-start | bytes 2228224 | tf_op jit(solution)/shard_map/reduce_scatter | solution.py:533
  129.4 1.7 copy-start.6
  131.0 306.8 %reduce-scatter.20.cloned.1.call-start = ((), (), s32[]{:S(2)}) async-start(), calls=%async_computation.15 | async-start | bytes 2228224 | tf_op jit(solution)/shard_map/reduce_scatter | solution.py:533
  132.8 369.7 %reduce-scatter.26.cloned.1.call-start = ((), (), s32[]{:S(2)}) async-start(), calls=%async_computation.18 | async-start | bytes 2228224 | tf_op jit(solution)/shard_map/reduce_scatter | solution.py:533
  132.8 3.2 copy-start.2
  136.0 451.0 %reduce-scatter.28.cloned.1.call-start = ((), (), s32[]{:S(2)}) async-start(), calls=%async_computation.19 | async-start | bytes 6127616 | tf_op jit(solution)/shard_map/reduce_scatter | solution.py:533
  138.9 1.9 copy-start.1
  138.9 532.8 %reduce-scatter.30.cloned.1.call-start = ((), (), s32[]{:S(2)}) async-start(), calls=%async_computation.20 | async-start | bytes 6127616 | tf_op jit(solution)/shard_map/reduce_scatter | solution.py:533
  143.6 1.8 copy-start
  143.7 612.7 %reduce-scatter.32.cloned.1.call-start = ((), (), s32[]{:S(2)}) async-start(), calls=%async_computation.21 | async-start | bytes 6127616 | tf_op jit(solution)/shard_map/reduce_scatter | solution.py:533
  148.8 746.1 %reduce-scatter.22.cloned.1.call-start = ((), (), s32[]{:S(2)}) async-start(), calls=%async_computation.16 | async-start | bytes 2162688 | tf_op jit(solution)/shard_map/reduce_scatter | solution.py:533
  151.6 879.6 %reduce-scatter.24.cloned.1.call-start = ((), (), s32[]{:S(2)}) async-start(), calls=%async_computation.17 | async-start | bytes 2162688 | tf_op jit(solution)/shard_map/reduce_scatter | solution.py:533
  151.7 1.8 copy-start.11
  151.7 1.8 copy-start.12
  151.7 1.8 copy-start.14
  (4 other events, 5.3 us)
Sparse Core Ops, SparseCore 0:
  126.2 57.8 reduce-scatter.13
  188.2 56.3 reduce-scatter.15
  248.4 60.5 reduce-scatter.11
  313.0 60.5 reduce-scatter.17
  377.2 60.5 reduce-scatter.19
  441.9 60.5 reduce-scatter.25
  506.4 80.5 reduce-scatter.27
  590.9 80.7 reduce-scatter.29
  675.6 80.7 reduce-scatter.31
  759.0 135.8 reduce-scatter.21
  897.8 133.4 reduce-scatter.23
